TPU v7x, 32 devices: a whole 2x2x4 slice. The times are simulated.
32 devices in a mesh: grp: 2 (over x), pair: 16 (over z, y, core).
Axes of the slice: x: 2, y: 2, z: 4, core: 2. Of those that a mesh axis runs over, the one named last changes fastest.
Arguments:
- three_center: bfloat16 [16, 3, 256, 4096], P('pair'), may hold values from -0.125 to 0.125
- block_mask: int32 [16, 3], P('pair'), may hold values 0 or 1
- green_occ: bfloat16 [16, 6, 4096], P('pair', 'grp'), parts along dimension 1, may hold values from -0.4375 to 0.4375
- green_virt: bfloat16 [16, 6, 4096], P('pair', 'grp'), parts along dimension 1, may hold values from -0.4375 to 0.4375
- green_mask: int32 [16, 3], P('pair'), may hold values 0 or 1
- block_of_slot: int32 [16], replicated, may hold values from 0 to 15, each once
Outputs:
- chi: float32 [256, 512], P('pair', 'grp'), parts along dimension 1
There are 2 independent parts, one for each index of `grp`. A program takes and returns all parts, laid end to end along the dimension named above; an argument that names none is the same for every part. Nothing has to cross between parts.
Inputs may be any that keep to these rules, and one draw needn't show every extreme that they name: `block_of_slot`: every atom block stands in exactly one slot.
All inputs are finite; a program needn't handle non-finite values. No bound on the sum of `block_mask` or of `green_mask` on one device may be relied on, other than what follows from the above.
Results may differ from a plain program's by a relative error of at most 0.004.
Values may be sent and summed in bfloat16 or wider, within the bound.
A program may use at most 128 MiB of HBM per device.

v0:
```python
import jax
import jax.numpy as jnp
from jax import lax
from jax.sharding import PartitionSpec as P

BS = 64
HB = 1
HG = 1
KN = 3
KG = 3


def invert(block_of_slot):
    amount = block_of_slot.shape[0]
    return (
        jnp.zeros((amount,), jnp.int32).at[block_of_slot].set(jnp.arange(amount, dtype=jnp.int32))
    )


def build_left(blocks, columns, gocc, block_count):
    lefts = []
    for target in range(-HB, HB + 1):
        middles = [m for m in range(HG, -HG - 1, -1) if abs(target - m) <= HB]
        green_cat = jnp.concatenate(
            [gocc[(columns + (target - m)) % block_count, m + HG] for m in middles], axis=2
        )
        lowest = target - middles[0] + HB
        tensor_cat = blocks[:, lowest : lowest + len(middles)]
        tensor_cat = tensor_cat.reshape(blocks.shape[0], len(middles) * BS, blocks.shape[3])
        lefts.append(
            jnp.einsum(
                "lij,ljq->liq", green_cat, tensor_cat, preferred_element_type=jnp.float32
            ).astype(jnp.bfloat16)
        )
    return jnp.stack(lefts, axis=1)


def build_right(left_turned, gvirt):
    rights = []
    count = left_turned.shape[0]
    for target in range(-HB, HB + 1):
        middles = [m for m in range(-HG, HG + 1) if abs(target - m) <= HB]
        virt_cat = gvirt[:, middles[0] + HG : middles[-1] + HG + 1].reshape(
            count, len(middles) * BS, BS
        )
        left_cat = jnp.concatenate(
            [jnp.roll(left_turned[:, target - m + HB], -m, axis=0) for m in middles], axis=1
        )
        rights.append(
            jnp.einsum(
                "ljk,ljq->lkq", virt_cat, left_cat, preferred_element_type=jnp.float32
            ).astype(jnp.bfloat16)
        )
    return jnp.stack(rights, axis=1)


def on_device(three_center, block_mask, green_occ, green_virt, green_mask, block_of_slot):
    aux_count = three_center.shape[2]
    block_count = block_of_slot.shape[0]
    local_aux = aux_count // lax.axis_size("pair")
    slot_of_block = invert(block_of_slot)
    masked = three_center * block_mask.astype(jnp.bfloat16)[:, :, None, None]
    green_keep = green_mask.astype(jnp.bfloat16)[:, :, None]
    every_occ, every_virt = (
        lax.all_gather(green_occ * green_keep, "pair", axis=0, tiled=True),
        lax.all_gather(green_virt * green_keep, "pair", axis=0, tiled=True),
    )
    gocc = every_occ[slot_of_block].reshape(block_count, KG, BS, BS)
    gvirt = every_virt[slot_of_block].reshape(block_count, KG, BS, BS)
    regrouped = lax.all_to_all(masked, "pair", split_axis=2, concat_axis=0, tiled=True)
    curve = regrouped[slot_of_block].reshape(block_count, KN, local_aux, BS, BS)
    curve = curve.transpose(0, 1, 3, 2, 4).reshape(block_count, KN, BS, local_aux * BS)
    left = build_left(curve, jnp.arange(block_count, dtype=jnp.int32), gocc, block_count)
    left = left.reshape(block_count, KN, BS, local_aux, BS)
    left_turned = left.transpose(0, 1, 4, 3, 2).reshape(block_count, KN, BS, local_aux * BS)
    right_turned = build_right(left_turned, gvirt)
    right = right_turned.reshape(block_count, KN, BS, local_aux, BS).transpose(0, 1, 3, 4, 2)
    right_slots = right.reshape(block_count, KN, local_aux, BS * BS)[block_of_slot]
    returned = lax.all_to_all(right_slots, "pair", split_axis=0, concat_axis=2, tiled=True)
    return lax.psum_scatter(
        lax.dot_general(
            masked, returned, (((0, 1, 3), (0, 1, 3)), ((), ())), preferred_element_type=jnp.float32
        ),
        "pair",
        scatter_dimension=0,
        tiled=True,
    )


def solution(mesh):
    return jax.shard_map(
        on_device,
        mesh=mesh,
        in_specs=(
            P("pair", None, None, None),
            P("pair", None),
            P("pair", "grp", None),
            P("pair", "grp", None),
            P("pair", None),
            P(),
        ),
        out_specs=P("pair", "grp"),
        check_vma=False,
    )
```

profile of v0, /device:TPU:0, one launch (start us, length us, event | category | flops | bytes accessed | tf_op | source)
XLA Modules:
  0.0 697.1 jit_solution(6099566690372054543)
XLA Ops:
  7.2 11.7 %copy_multiply_fusion = bf16[1,3,256,4096]{3,1,0,2:T(4,128)(2,1)} fusion(bf16[1,3,256,4096]{3,2,1,0:T(8,128)(2,1)} %param.6, bf16[3]{0:T(256)(128)(2,1)S(1)} %convert_bitcast_fusion.1), kind=kLoop, calls=%fused_computation.14 | loop fusion | flops 3145728 | bytes 12582918 | tf_op jit(solution)/shard_map/mul | solution.py:62
  18.9 7.6 %all-to-all-start = ((bf16[1,3,256,4096]{3,1,0,2:T(4,128)(2,1)}), bf16[1,3,256,4096]{3,1,0,2:T(4,128)(2,1)}, u32[]{:S(2)}, u32[]{:S(2)}) async-start(bf16[1,3,256,4096]{3,1,0,2:T(4,128)(2,1)} %copy_multiply_fusion), calls=%async_computation | async-start | bytes 16777216 | tf_op jit(solution)/shard_map/all_to_all | solution.py:70
  27.4 166.6 %all_gather.6 = bf16[16,3,4096]{2,1,0:T(4,128)(2,1)S(1)} all-gather(bf16[1,3,4096]{2,1,0:T(4,128)(2,1)S(1)} %get-tuple-element.21), channel_id=1, replica_groups=mesh['grp'=2,'pair'=16] {'pair'}, dimensions={0}, use_global_device_ids=true | all-gather | bytes 417792 | tf_op jit(solution)/shard_map/all_gather | solution.py:66
  196.8 48.0 %all_gather.7 = bf16[16,3,4096]{2,1,0:T(4,128)(2,1)S(1)} all-gather(bf16[1,3,4096]{2,1,0:T(4,128)(2,1)S(1)} %get-tuple-element.20), channel_id=1, replica_groups=mesh['grp'=2,'pair'=16] {'pair'}, dimensions={0}, use_global_device_ids=true | all-gather | bytes 417792 | tf_op jit(solution)/shard_map/all_gather | solution.py:65
  256.7 11.2 %copy.106 = bf16[1,3,16,16,4096]{4,3,1,2,0:T(8,128)(2,1)} copy(bf16[1,3,16,16,4096]{4,1,3,2,0:T(4,128)(2,1)} %bitcast.5) | data formatting | bytes 12582912 | tf_op jit(solution)/shard_map/all_to_all | solution.py:70
  267.8 6.4 gather_fusion.4
  274.2 17.9 %reshape.198 = bf16[16,3,16,64,64]{4,3,2,1,0:T(8,128)(2,1)} reshape(bf16[16,3,16,4096]{3,2,1,0:T(8,128)(2,1)} %gather_fusion.4) | data formatting | bytes 12582912 | tf_op jit(solution)/shard_map/reshape | solution.py:71
  292.2 15.5 %copy.78 = bf16[16,3,64,16,64]{4,3,2,1,0:T(8,128)(2,1)} copy(bf16[16,3,64,16,64]{4,2,3,1,0:T(8,128)(2,1)} %bitcast.95) | data formatting | bytes 12582912 | tf_op jit(solution)/shard_map/transpose | solution.py:72
  307.6 17.2 %reshape_reshape.6 = bf16[16,192,1024]{2,1,0:T(8,128)(2,1)} reshape(bf16[16,3,64,16,64]{4,3,2,1,0:T(8,128)(2,1)} %copy.78) | data formatting | bytes 12582912 | tf_op jit(solution)/shard_map/reshape;reshape | solution.py:29
  324.9 17.2 %reshape.199 = bf16[16,3,64,1024]{3,2,1,0:T(8,128)(2,1)} reshape(bf16[16,3,64,16,64]{4,3,2,1,0:T(8,128)(2,1)} %copy.78) | data formatting | bytes 12582912 | tf_op jit(solution)/shard_map/reshape | solution.py:72
  346.2 4.4 stack.25
  350.7 5.4 fusion.65
  367.8 11.3 %maximum_bitcast_fusion = bf16[16,3,64,16,64]{2,3,4,0,1:T(8,128)(2,1)} fusion(bf16[16,1,64,16,64]{4,3,2,0,1:T(8,128)(2,1)} %stack.26, bf16[16,1,64,16,64]{4,3,2,0,1:T(8,128)(2,1)} %stack.25, bf16[16,1,64,16,64]{4,3,2,0,1:T(8,128)(2,1)} %stack.24), kind=kLoop, calls=%fused_computation.12 | loop fusion | flops 6291456 | bytes 12582912 | tf_op jit(solution)/shard_map/transpose | solution.py:75
  379.1 21.8 %copy.80 = bf16[16,3,64,16,64]{4,3,2,0,1:T(8,128)(2,1)} copy(bf16[16,3,64,16,64]{2,3,4,0,1:T(8,128)(2,1)} %maximum_bitcast_fusion) | data formatting | bytes 12582912 | tf_op jit(solution)/shard_map/transpose | solution.py:75
  400.9 17.2 %reshape.202 = bf16[16,3,64,1024]{3,2,0,1:T(8,128)(2,1)} reshape(bf16[16,3,64,16,64]{4,3,2,0,1:T(8,128)(2,1)} %copy.80) | data formatting | bytes 12582912 | tf_op jit(solution)/shard_map/reshape | solution.py:75
  418.2 6.0 slice_bitcast_fusion.6
  445.6 10.0 %maximum_bitcast_fusion.1 = bf16[16,3,16,64,64]{4,3,2,1,0:T(8,128)(2,1)} fusion(bf16[16,1,64,16,64]{2,4,3,1,0:T(8,128)(2,1)} %bitcast.99, bf16[16,1,64,16,64]{2,4,3,1,0:T(8,128)(2,1)} %bitcast.98, bf16[16,1,64,16,64]{2,4,3,1,0:T(8,128)(2,1)} %bitcast.97), kind=kLoop, calls=%fused_computation.13 | loop fusion | flops 6291456 | bytes 12582912 | tf_op jit(solution)/shard_map/transpose | solution.py:77
  455.6 17.0 %reshape.204 = bf16[16,3,16,4096]{3,2,1,0:T(8,128)(2,1)} reshape(bf16[16,3,16,64,64]{4,3,2,1,0:T(8,128)(2,1)} %maximum_bitcast_fusion.1) | data formatting | bytes 12582912 | tf_op jit(solution)/shard_map/reshape | solution.py:78
  472.6 6.4 gather_fusion.10
  479.0 4.6 all-to-all-start.1
  483.9 11.7 %fusion.74 = bf16[3,256,4096]{2,0,1:T(4,128)(2,1)} fusion(bf16[3]{0:T(256)(128)(2,1)S(1)} %convert_bitcast_fusion.1, bf16[1,3,256,4096]{3,2,1,0:T(8,128)(2,1)} %param.6), kind=kLoop, calls=%fused_computation.112 | loop fusion | flops 3145728 | bytes 12582918 | tf_op jit(solution)/shard_map/reshape.11
  495.6 102.2 %all-to-all-done.1 = bf16[16,3,16,4096]{3,2,1,0:T(8,128)(2,1)} async-done(((bf16[16,3,16,4096]{3,2,1,0:T(8,128)(2,1)}), bf16[16,3,16,4096]{3,2,1,0:T(8,128)(2,1)}, u32[]{:S(2)}, u32[]{:S(2)}) %all-to-all-start.1) | async-done | bytes 6291488 | tf_op jit(solution)/shard_map/all_to_all | solution.py:79
  603.0 8.2 %fusion.33 = f32[256,256]{1,0:T(8,128)} fusion(bf16[3,256,4096]{2,1,0:T(8,128)(2,1)S(1)} %bitcast.102, bf16[3,256,4096]{2,0,1:T(4,128)(2,1)S(1)} %copy-done.1), kind=kOutput, calls=%fused_computation.53 | convolution fusion | flops 1610612736 | bytes 12845056 | tf_op jit(solution)/shard_map/dot_general | solution.py:81
  611.2 78.8 %reduce-scatter.2.cloned.1.call-done = f32[16,256]{1,0:T(8,128)} async-done(((f32[256,256]{1,0:T(8,128)}), f32[16,256]{1,0:T(8,128)}) %reduce-scatter.2.cloned.1.call-update) | async-done | bytes 16400 | tf_op jit(solution)/shard_map/reduce_scatter | solution.py:80
  (74 shorter events, 58.8 us)
Async XLA Ops:
  18.9 7.6 %copy-start.9 = (s32[16]{0:T(128)S(1)}, s32[16]{0:T(128)}, u32[]{:S(2)}) copy-start(s32[16]{0:T(128)} %param.11) | copy-start | bytes 196
  18.9 8.3 %copy-start.10 = (s32[1,3]{1,0:T(1,128)S(1)}, s32[1,3]{1,0:T(1,128)}, u32[]{:S(2)}) copy-start(s32[1,3]{1,0:T(1,128)} %param.10) | copy-start | bytes 40
  18.9 8.3 %copy-start.7 = (bf16[1,3,4096]{2,1,0:T(4,128)(2,1)S(1)}, bf16[1,3,4096]{2,1,0:T(4,128)(2,1)}, u32[]{:S(2)}) copy-start(bf16[1,3,4096]{2,1,0:T(4,128)(2,1)} %param.8) | copy-start | bytes 73732
  18.9 8.3 %copy-start.8 = (bf16[1,3,4096]{2,1,0:T(4,128)(2,1)S(1)}, bf16[1,3,4096]{2,1,0:T(4,128)(2,1)}, u32[]{:S(2)}) copy-start(bf16[1,3,4096]{2,1,0:T(4,128)(2,1)} %param.9) | copy-start | bytes 73732
  18.9 237.7 %all-to-all-start = ((bf16[1,3,256,4096]{3,1,0,2:T(4,128)(2,1)}), bf16[1,3,256,4096]{3,1,0,2:T(4,128)(2,1)}, u32[]{:S(2)}, u32[]{:S(2)}) async-start(bf16[1,3,256,4096]{3,1,0,2:T(4,128)(2,1)} %copy_multiply_fusion), calls=%async_computation | async-start | bytes 16777216 | tf_op jit(solution)/shard_map/all_to_all | solution.py:70
  350.6 5.4 copy-start.3
  356.1 4.8 copy-start.2
  418.2 7.2 %copy-start = (bf16[16,3,64,1024]{3,2,0,1:T(8,128)(2,1)S(1)}, bf16[16,3,64,1024]{3,2,0,1:T(8,128)(2,1)}, u32[]{:S(2)}) copy-start(bf16[16,3,64,1024]{3,2,0,1:T(8,128)(2,1)} %reshape.202) | copy-start | bytes 18874372
  425.4 3.2 copy-start.6
  428.6 4.1 copy-start.4
  436.3 3.2 copy-start.5
  479.0 118.8 %all-to-all-start.1 = ((bf16[16,3,16,4096]{3,2,1,0:T(8,128)(2,1)}), bf16[16,3,16,4096]{3,2,1,0:T(8,128)(2,1)}, u32[]{:S(2)}, u32[]{:S(2)}) async-start(bf16[16,3,16,4096]{3,2,1,0:T(8,128)(2,1)} %gather_fusion.10), calls=%async_computation.1 | async-start | bytes 12582912 | tf_op jit(solution)/shard_map/all_to_all | solution.py:79
  483.7 206.3 %reduce-scatter.2.cloned.1.call-start = ((), (), s32[]{:S(2)}) async-start(), calls=%async_computation.3 | async-start | bytes 278528 | tf_op jit(solution)/shard_map/reduce_scatter | solution.py:80
  597.8 5.2 copy-start.1
Sparse Core Ops, SparseCore 0:
  611.3 78.6 reduce-scatter.1
where the time goes:
time: 709 us; the launch traced here: 697 us
  blocking collectives  215 us (30%)
  local copies, waits for them, and re-layouts  206 us (29%)
  waiting for transfers between devices  181 us (26%)
  other arithmetic  45.6 us (6%)
  matrix products  23.3 us (3%)
  between operations  13.9 us (2%)
  starting transfers between devices  12.4 us (2%)
    all_gather x1, blocking collectives, on_device(): lax.all_gather(green_virt * green_keep, 'pair', axis=0, tiled=True)  167 us
    all_to_all x1, waiting for transfers between devices, on_device(): lax.all_to_all(right_slots, 'pair', split_axis=0, concat_axis=2, tiled=True)  102 us
    reduce_scatter x1, waiting for transfers between devices, on_device(): lax.psum_scatter(lax.dot_general(masked, returned, (((0, 1, 3), (0, 1, 3)...  78.8 us
    all_gather x1, blocking collectives, on_device(): lax.all_gather(green_occ * green_keep, 'pair', axis=0, tiled=True)  48 us
    transpose x1, local copies, waits for them, and re-layouts, on_device(): left.transpose(0, 1, 4, 3, 2).reshape(block_count, KN, BS, local_aux * BS)  21.8 us
    reshape x1, local copies, waits for them, and re-layouts, on_device(): curve = regrouped[slot_of_block].reshape(block_count, KN, local_aux, BS, BS)  17.9 us
    reshape x1, local copies, waits for them, and re-layouts, on_device(): curve.transpose(0, 1, 3, 2, 4).reshape(block_count, KN, BS, local_aux * BS)  17.2 us
    another operation x1, local copies, waits for them, and re-layouts, build_left(): tensor_cat.reshape(blocks.shape[0], len(middles) * BS, blocks.shape[3])  17.2 us
  transfers between devices with their start and end apart: 3, of which 2 were waited for; matrix products, arithmetic and copies ran while one was open for 4% of the time, Pallas kernels for 0%

commit v1 on v0

--- a/solution.py
+++ b/solution.py
@@ -1,6 +1,10 @@
+import functools
+
 import jax
 import jax.numpy as jnp
 from jax import lax
+from jax.experimental import pallas as pl
+from jax.experimental.pallas import tpu as pltpu
 from jax.sharding import PartitionSpec as P
 
 BS = 64
@@ -8,6 +12,7 @@
 HG = 1
 KN = 3
 KG = 3
+MESH = pl.DeviceIdType.MESH
 
 
 def invert(block_of_slot):
@@ -87,9 +92,299 @@
     )
 
 
+def row_sliced(n):
+    return BS % n == 0 and (BS // n) * BS % 128 == 0
+
+
+def greet(n, me):
+    barrier = pltpu.get_barrier_semaphore()
+
+    def hello(k, carry):
+        pl.semaphore_signal(
+            barrier, inc=1, device_id={"pair": lax.rem(me + k, n)}, device_id_type=MESH
+        )
+        return carry
+
+    lax.fori_loop(1, n, hello, 0)
+    pl.semaphore_wait(barrier, n - 1)
+
+
+def gather_kernel(n, own_ref, every_ref, send_sem, recv_sem, local_sem):
+    me = lax.axis_index("pair")
+    greet(n, me)
+    local = pltpu.make_async_copy(own_ref, every_ref.at[me], local_sem)
+    local.start()
+
+    def send_of(k):
+        return pltpu.make_async_remote_copy(
+            src_ref=own_ref,
+            dst_ref=every_ref.at[me],
+            send_sem=send_sem.at[k],
+            recv_sem=recv_sem.at[k],
+            device_id={"pair": lax.rem(me + k, n)},
+            device_id_type=MESH,
+        )
+
+    def start(k, carry):
+        send_of(k).start()
+        return carry
+
+    def finish(k, carry):
+        copy = send_of(k)
+        copy.wait_recv()
+        copy.wait_send()
+        return carry
+
+    lax.fori_loop(1, n, start, 0)
+    lax.fori_loop(1, n, finish, 0)
+    local.wait()
+
+
+def gather_small(own, n):
+    return pl.pallas_call(
+        functools.partial(gather_kernel, n),
+        out_shape=jax.ShapeDtypeStruct((n,) + own.shape, own.dtype),
+        in_specs=[pl.BlockSpec(memory_space=pltpu.VMEM)],
+        out_specs=pl.BlockSpec(memory_space=pltpu.VMEM),
+        scratch_shapes=[
+            pltpu.SemaphoreType.DMA((n,)),
+            pltpu.SemaphoreType.DMA((n,)),
+            pltpu.SemaphoreType.DMA,
+        ],
+        compiler_params=pltpu.CompilerParams(collective_id=0, has_side_effects=True),
+        name="gather_greens",
+    )(own)
+
+
+def scatter_kernel(n, part_ref, out_ref, landed, send_sem, recv_sem):
+    me = lax.axis_index("pair")
+    rows = out_ref.shape[0]
+    greet(n, me)
+
+    def send_of(k):
+        to = lax.rem(me + k, n)
+        return pltpu.make_async_remote_copy(
+            src_ref=part_ref.at[pl.ds(pl.multiple_of(to * rows, rows), rows)],
+            dst_ref=landed.at[k],
+            send_sem=send_sem.at[k],
+            recv_sem=recv_sem.at[k],
+            device_id={"pair": to},
+            device_id_type=MESH,
+        )
+
+    def start(k, carry):
+        send_of(k).start()
+        return carry
+
+    def finish(k, carry):
+        copy = send_of(k)
+        copy.wait_recv()
+        copy.wait_send()
+        return carry
+
+    lax.fori_loop(1, n, start, 0)
+    lax.fori_loop(1, n, finish, 0)
+    total = part_ref[pl.ds(pl.multiple_of(me * rows, rows), rows), :]
+    for k in range(1, n):
+        total = total + landed[k]
+    out_ref[...] = total
+
+
+def scatter_sum(part, n):
+    rows = part.shape[0] // n
+    return pl.pallas_call(
+        functools.partial(scatter_kernel, n),
+        out_shape=jax.ShapeDtypeStruct((rows, part.shape[1]), jnp.float32),
+        in_specs=[pl.BlockSpec(memory_space=pltpu.VMEM)],
+        out_specs=pl.BlockSpec(memory_space=pltpu.VMEM),
+        scratch_shapes=[
+            pltpu.VMEM((n, rows, part.shape[1]), jnp.float32),
+            pltpu.SemaphoreType.DMA((n,)),
+            pltpu.SemaphoreType.DMA((n,)),
+        ],
+        compiler_params=pltpu.CompilerParams(collective_id=1, has_side_effects=True),
+        name="scatter_chi",
+    )(part)
+
+
+def swap_major(chunks):
+    return jnp.swapaxes(jnp.stack(chunks, axis=0), 0, 1)
+
+
+def left_kernel(green_ref, tensor_ref, left_ref):
+    count = tensor_ref.shape[2]
+    half = count // 2
+    pairs = BS * BS // 128
+    low = lax.broadcasted_iota(jnp.int32, (half, pairs, 128), 2) < BS
+    rows = []
+    for a in range(KN):
+        x = swap_major([tensor_ref[0, a, :, 128 * t : 128 * (t + 1)] for t in range(pairs)])
+        first, second = x[:half], x[half:]
+        even = jnp.where(low, first, pltpu.roll(second, BS, 2))
+        odd = jnp.where(low, pltpu.roll(first, BS, 2), second)
+        for y in (even, odd):
+            rows.append(jnp.concatenate([y[p] for p in range(half)], axis=1))
+    stacked = jnp.concatenate(rows, axis=0)
+    result = jnp.dot(green_ref[...], stacked, preferred_element_type=jnp.float32)
+    result = result.astype(jnp.bfloat16)
+    for a in range(KN):
+        base = a * BS
+        even = jnp.stack(
+            [result[base : base + pairs, 128 * p : 128 * (p + 1)] for p in range(half)], axis=0
+        )
+        odd = jnp.stack(
+            [result[base + pairs : base + BS, 128 * p : 128 * (p + 1)] for p in range(half)],
+            axis=0,
+        )
+        first = jnp.where(low, even, pltpu.roll(odd, BS, 2))
+        second = jnp.where(low, pltpu.roll(even, BS, 2), odd)
+        back = jnp.swapaxes(jnp.concatenate([first, second], axis=0), 0, 1)
+        for t in range(pairs):
+            left_ref[0, a, :, 128 * t : 128 * (t + 1)] = back[t]
+
+
+def left_products(tensor, green, chunk=32):
+    aux = tensor.shape[2]
+    spec = pl.BlockSpec((1, KN, chunk, BS * BS), lambda q: (0, 0, q, 0))
+    return pl.pallas_call(
+        left_kernel,
+        grid=(aux // chunk,),
+        out_shape=jax.ShapeDtypeStruct(tensor.shape, jnp.bfloat16),
+        in_specs=[pl.BlockSpec((KN * BS, KN * BS), lambda q: (0, 0)), spec],
+        out_specs=spec,
+        compiler_params=pltpu.CompilerParams(vmem_limit_bytes=48 * 1024 * 1024),
+        cost_estimate=pl.CostEstimate(
+            flops=2 * 9 * BS * BS * BS * aux,
+            bytes_accessed=4 * KN * aux * BS * BS,
+            transcendentals=0,
+        ),
+        name="left_products",
+    )(green, tensor)
+
+
+def chi_kernel(slot_ref, mask_ref, before_ref, here_ref, after_ref, tensor_ref, virt_ref, chi_ref):
+    lam = pl.program_id(0)
+    width = tensor_ref.shape[3]
+    rows = width // BS
+    lefts = (before_ref, here_ref, after_ref)
+    line = lax.broadcasted_iota(jnp.int32, (width, width), 0) // BS
+    column = lax.broadcasted_iota(jnp.int32, (width, width), 1) // BS
+    spread = []
+    for c in range(KG):
+        block = jnp.concatenate([virt_ref[0, c]] * rows, axis=1)
+        block = jnp.concatenate([block] * rows, axis=0)
+        spread.append(jnp.where(line == column, block, jnp.zeros_like(block)))
+    total = jnp.zeros(chi_ref.shape, jnp.float32)
+    for a in range(-HB, HB + 1):
+        right = jnp.zeros((tensor_ref.shape[2], width), jnp.float32)
+        for c in range(-HG, HG + 1):
+            if abs(a - c) <= HB:
+                right = right + jnp.dot(
+                    lefts[c + HG][0, a - c + HB],
+                    spread[c + HG],
+                    preferred_element_type=jnp.float32,
+                )
+        keep = mask_ref[slot_ref[lam] * KN + a + HB].astype(jnp.float32)
+        right = (right * keep).astype(jnp.bfloat16)
+        total = total + lax.dot_general(
+            tensor_ref[0, a + HB],
+            right,
+            (((1,), (1,)), ((), ())),
+            preferred_element_type=jnp.float32,
+        )
+
+    @pl.when(lam == 0)
+    def _():
+        chi_ref[...] = total
+
+    @pl.when(lam != 0)
+    def _():
+        chi_ref[...] += total
+
+
+def chi_partial(slot_of_block, every_mask, left, tensor, virt):
+    n, _, aux, width = tensor.shape
+
+    def at(shift):
+        return pl.BlockSpec(
+            (1, KN, aux, width),
+            lambda lam, slot, mask: (slot[lax.rem(lam + shift + n, n)], 0, 0, 0),
+        )
+
+    return pl.pallas_call(
+        chi_kernel,
+        grid_spec=pltpu.PrefetchScalarGridSpec(
+            num_scalar_prefetch=2,
+            grid=(n,),
+            in_specs=[
+                at(-1),
+                at(0),
+                at(1),
+                at(0),
+                pl.BlockSpec((1, KG, BS, BS), lambda lam, slot, mask: (slot[lam], 0, 0, 0)),
+            ],
+            out_specs=pl.BlockSpec((aux, aux), lambda lam, slot, mask: (0, 0)),
+        ),
+        out_shape=jax.ShapeDtypeStruct((aux, aux), jnp.float32),
+        compiler_params=pltpu.CompilerParams(vmem_limit_bytes=48 * 1024 * 1024),
+        cost_estimate=pl.CostEstimate(
+            flops=2 * n * aux * width * (7 * width + KN * aux),
+            bytes_accessed=8 * n * KN * aux * width,
+            transcendentals=0,
+        ),
+        name="chi_partial",
+    )(slot_of_block, every_mask, left, left, left, tensor, virt)
+
+
+def green_matrix(gocc, every_mask, slot_of_block, column):
+    n = slot_of_block.shape[0]
+    keep = every_mask[slot_of_block[column]].astype(jnp.bfloat16)
+    zero = jnp.zeros((BS, BS), jnp.bfloat16)
+    lines = []
+    for target in range(-HB, HB + 1):
+        line = []
+        for source in range(-HB, HB + 1):
+            step = target - source
+            if abs(step) <= HG:
+                slot = slot_of_block[(column + source + n) % n]
+                line.append(gocc[slot, step + HG] * keep[source + HB])
+            else:
+                line.append(zero)
+        lines.append(jnp.concatenate(line, axis=1))
+    whole = jnp.concatenate(lines, axis=0).reshape(KN, BS // 2, 2, KN, BS // 2, 2)
+    return whole.transpose(0, 2, 1, 3, 5, 4).reshape(KN * BS, KN * BS)
+
+
+def by_rows(array, n):
+    _, blocks, aux, cells = array.shape
+    moved = lax.all_to_all(array, "pair", split_axis=3, concat_axis=0, tiled=True)
+    return moved.reshape(n, blocks, aux, cells // n)
+
+
+def by_row_slices(three_center, block_mask, green_occ, green_virt, green_mask, block_of_slot):
+    n = lax.axis_size("pair")
+    slot_of_block = invert(block_of_slot)
+    green_keep = green_mask.astype(jnp.bfloat16)[:, :, None]
+    greens = jnp.concatenate([green_occ * green_keep, green_virt * green_keep], axis=1)
+    greens = greens.reshape(16, 2 * KG * BS * BS // 16)
+    mask = jnp.zeros((16, 128), jnp.bfloat16).at[0, :KN].set(block_mask[0].astype(jnp.bfloat16))
+    every = gather_small(jnp.concatenate([greens, mask], axis=1), n)
+    tensor_rows = by_rows(three_center, n)
+    every_mask = every[:, 0, greens.shape[1] : greens.shape[1] + KN].astype(jnp.int32)
+    every_green = every[:, :, : greens.shape[1]].reshape(n, 2, KG, BS, BS)
+    column = block_of_slot[lax.axis_index("pair")]
+    green = green_matrix(every_green[:, 0], every_mask, slot_of_block, column)
+    left = left_products(three_center, green)
+    left_rows = by_rows(left, n)
+    part = chi_partial(
+        slot_of_block, every_mask.reshape(-1), left_rows, tensor_rows, every_green[:, 1]
+    )
+    return scatter_sum(part, n)
+
+
 def solution(mesh):
     return jax.shard_map(
-        on_device,
+        by_row_slices if row_sliced(mesh.shape["pair"]) else on_device,
         mesh=mesh,
         in_specs=(
             P("pair", None, None, None),

time: 709 us -> 512 us (0.72); the launches traced: 697 us -> 509 us
  blocking collectives: 215 us -> 0 us
  local copies, waits for them, and re-layouts: 206 us -> 76.3 us
  Pallas kernels: 0 us -> 94.2 us
  waiting for transfers between devices: 181 us -> 274 us
  other arithmetic: 45.6 us -> 7 us
  starting transfers between devices: 12.4 us -> 46.2 us
  matrix products: 23.3 us -> 0 us
    all_gather x2 -> x0, blocking collectives: 215 us -> none  [the longest x1 167 us: on_device(): lax.all_gather(green_virt * green_keep, 'pair', axis=0, tiled=True)]
    all_to_all x2, waiting for transfers between devices: 102 us -> 274 us  [by_rows(): lax.all_to_all(array, 'pair', split_axis=3, concat_axis=0, tiled=True)]
    pallas_call x0 -> x4, Pallas kernels: none -> 94.2 us  [the longest x1 41.8 us: scatter_sum(): pl.pallas_call(functools.partial(scatter_kernel, n), out_shape=jax.ShapeD...]
    reduce_scatter x1 -> x0, waiting for transfers between devices: 78.8 us -> none  [on_device(): lax.psum_scatter(lax.dot_general(masked, returned, (((0, 1, 3), (0, 1, 3)...]
    reshape x8 -> x4, local copies, waits for them, and re-layouts: 73 us -> 12.1 us  [the longest x1 10.9 us: green_matrix(): jnp.concatenate(lines, axis=0).reshape(KN, BS // 2, 2, KN, BS // 2, 2)]
    another operation x8 -> x0, local copies, waits for them, and re-layouts: 40.8 us -> none  [the longest x1 17.2 us: build_left(): tensor_cat.reshape(blocks.shape[0], len(middles) * BS, blocks.shape[3])]
    all_to_all x2, starting transfers between devices: 12.2 us -> 46.2 us  [by_rows(): lax.all_to_all(array, 'pair', split_axis=3, concat_axis=0, tiled=True)]
    transpose x2 -> x1, local copies, waits for them, and re-layouts: 37.3 us -> 5.38 us  [green_matrix(): return whole.transpose(0, 2, 1, 3, 5, 4).reshape(KN * BS, KN * BS)]
  transfers between devices with their start and end apart: 3 -> 2, of which waited for: 2 -> 2; matrix products, arithmetic and copies ran while one was open for 4% -> 5% of each run, Pallas kernels for 0% -> 0%
where the time goes in v1:
time: 512 us; the launch traced here: 509 us
  waiting for transfers between devices  274 us (54%)
  Pallas kernels  94.2 us (18%)
  local copies, waits for them, and re-layouts  76.3 us (15%)
  starting transfers between devices  46.2 us (9%)
  between operations  11.1 us (2%)
  other arithmetic  7 us (1%)
    all_to_all x2, waiting for transfers between devices, by_rows(): lax.all_to_all(array, 'pair', split_axis=3, concat_axis=0, tiled=True)  274 us
    all_to_all x2, starting transfers between devices, by_rows(): lax.all_to_all(array, 'pair', split_axis=3, concat_axis=0, tiled=True)  46.2 us
    pallas_call x1, Pallas kernels, scatter_sum(): pl.pallas_call(functools.partial(scatter_kernel, n), out_shape=jax.ShapeD...  41.8 us
    all_to_all x2, local copies, waits for them, and re-layouts, by_rows(): lax.all_to_all(array, 'pair', split_axis=3, concat_axis=0, tiled=True)  26 us
    pallas_call x1, Pallas kernels, gather_small(): pl.pallas_call(functools.partial(gather_kernel, n), out_shape=jax.ShapeDt...  22.4 us
    pallas_call x1, Pallas kernels, chi_partial(): pl.pallas_call(chi_kernel, grid_spec=pltpu.PrefetchScalarGridSpec(num_sca...  19.3 us
    unnamed x4, local copies, waits for them, and re-layouts  15.1 us
    pallas_call x1, local copies, waits for them, and re-layouts, left_products(): pl.pallas_call(left_kernel, grid=(aux // chunk,), out_shape=jax.ShapeDtyp...  13.1 us
  transfers between devices with their start and end apart: 2, of which 2 were waited for; matrix products, arithmetic and copies ran while one was open for 5% of the time, Pallas kernels for 0%

profile of v1, /device:TPU:0, one launch (start us, length us, event | category | flops | bytes accessed | tf_op | source)
XLA Modules:
  0.0 509.2 jit_solution(8339990792263359193)
XLA Ops:
  0.0 1.2 dynamic_slice.43
  5.9 0.7 fusion.8
  12.9 0.9 broadcast_multiply_fusion.1
  14.5 22.4 %gather_greens.1 = bf16[16,16,1664]{2,1,0:T(8,128)(2,1)} custom-call(bf16[16,1664]{1,0:T(8,128)(2,1)} %fusion.1.own_ref), custom_call_target="tpu_custom_call" | custom-call | tf_op jit(solution)/shard_map/gather_greens/pallas_call | solution.py:144
  36.9 0.8 slice_convert_fusion
  37.7 1.2 slice.45
  40.2 0.9 reshape.86
  43.2 1.8 multiply_bitcast_fusion.6
  45.1 10.9 %reshape.87 = bf16[3,32,2,3,32,2]{5,4,3,2,1,0:T(8,128)(2,1)} reshape(bf16[192,192]{1,0:T(8,128)(2,1)S(1)} %maximum_maximum_fusion) | data formatting | bytes 147456 | tf_op jit(solution)/shard_map/reshape | solution.py:354
  56.0 5.4 %copy.21 = bf16[3,2,32,3,2,32]{5,4,3,2,1,0:T(2,128)(2,1)S(1)} copy(bf16[3,2,32,3,2,32]{4,5,3,1,2,0:T(8,128)(2,1)} %bitcast.44) | data formatting | bytes 147456 | tf_op jit(solution)/shard_map/transpose | solution.py:355
  61.6 10.7 %left_products.1 = bf16[1,3,256,4096]{3,2,1,0:T(8,128)(2,1)} custom-call(bf16[192,192]{1,0:T(8,128)(2,1)S(1)} %reshape.88.green_ref, bf16[1,3,256,4096]{3,2,1,0:T(8,128)(2,1)} %tensor_ref.1), custom_call_target="tpu_custom_call" | custom-call | flops 1207959552 | bytes 12582912 | tf_op jit(solution)/shard_map/left_products/pallas_call | solution.py:249
  72.3 13.1 %copy.22 = bf16[1,3,256,4096]{2,1,0,3:T(4,128)(2,1)} copy(bf16[1,3,256,4096]{3,2,1,0:T(8,128)(2,1)} %left_products.1) | data formatting | bytes 12582912 | tf_op jit(solution)/shard_map/left_products/pallas_call | solution.py:249
  85.4 9.7 %all-to-all-start = ((bf16[1,3,256,4096]{2,1,0,3:T(4,128)(2,1)}), bf16[1,3,256,4096]{2,1,0,3:T(4,128)(2,1)}, u32[]{:S(2)}, u32[]{:S(2)}) async-start(bf16[1,3,256,4096]{2,1,0,3:T(4,128)(2,1)} %copy.22), calls=%async_computation | async-start | bytes 16777216 | tf_op jit(solution)/shard_map/all_to_all | solution.py:360
  95.1 13.1 %copy.25 = bf16[1,3,256,4096]{2,1,0,3:T(4,128)(2,1)} copy(bf16[1,3,256,4096]{3,2,1,0:T(8,128)(2,1)} %tensor_ref.1) | data formatting | bytes 12582912 | tf_op args[0]
  108.2 137.6 %all-to-all-done = bf16[1,3,256,4096]{2,1,0,3:T(4,128)(2,1)} async-done(((bf16[1,3,256,4096]{2,1,0,3:T(4,128)(2,1)}), bf16[1,3,256,4096]{2,1,0,3:T(4,128)(2,1)}, u32[]{:S(2)}, u32[]{:S(2)}) %all-to-all-start) | async-done | bytes 6291488 | tf_op jit(solution)/shard_map/all_to_all | solution.py:360
  245.8 36.5 %all-to-all-start.1 = ((bf16[1,3,256,4096]{2,1,0,3:T(4,128)(2,1)}), bf16[1,3,256,4096]{2,1,0,3:T(4,128)(2,1)}, u32[]{:S(2)}, u32[]{:S(2)}) async-start(bf16[1,3,256,4096]{2,1,0,3:T(4,128)(2,1)} %copy.25), calls=%async_computation.1 | async-start | bytes 16777216 | tf_op jit(solution)/shard_map/all_to_all | solution.py:360
  282.4 0.8 fusion.6
  283.3 13.0 %copy.24 = bf16[1,3,256,16,256]{4,2,1,3,0:T(8,128)(2,1)} copy(bf16[1,3,256,16,256]{2,1,4,3,0:T(4,128)(2,1)} %bitcast.18) | data formatting | bytes 12582912 | tf_op jit(solution)/shard_map/all_to_all | solution.py:360
  296.3 136.8 %all-to-all-done.1 = bf16[1,3,256,4096]{2,1,0,3:T(4,128)(2,1)} async-done(((bf16[1,3,256,4096]{2,1,0,3:T(4,128)(2,1)}), bf16[1,3,256,4096]{2,1,0,3:T(4,128)(2,1)}, u32[]{:S(2)}, u32[]{:S(2)}) %all-to-all-start.1) | async-done | bytes 6291488 | tf_op jit(solution)/shard_map/all_to_all | solution.py:360
  433.1 13.0 %copy.27 = bf16[1,3,256,16,256]{4,2,1,3,0:T(8,128)(2,1)} copy(bf16[1,3,256,16,256]{2,1,4,3,0:T(4,128)(2,1)} %bitcast.21) | data formatting | bytes 12582912 | tf_op jit(solution)/shard_map/all_to_all | solution.py:360
  446.1 19.3 %chi_partial.1.part_ref = f32[256,256]{1,0:T(8,128)S(1)} custom-call(s32[16]{0:T(128)S(1)} %scatter_custom_fusion.slot_ref, s32[48]{0:T(128)S(1)} %reshape.89.mask_ref, bf16[16,3,256,256]{3,2,1,0:T(8,128)(2,1)} %bitcast.40, bf16[16,3,256,256]{3,2,1,0:T(8,128)(2,1)} %bitcast.41, bf16[16,3,256,256]{3,2,1,0:T(8,128)(2,1)} %bitcast.42, ...), custom_call_target="tpu_custom_call" | custom-call | flops 5368709120 | bytes 25165824 | tf_op jit(solution)/shard_map/chi_partial/pallas_call | solution.py:314
  465.4 0.7 copy-done
  466.1 41.8 %scatter_chi.1 = f32[16,256]{1,0:T(8,128)} custom-call(f32[256,256]{1,0:T(8,128)} %copy-done), custom_call_target="tpu_custom_call" | custom-call | tf_op jit(solution)/shard_map/scatter_chi/pallas_call | solution.py:195
  507.9 1.3 copy.35
  (16 shorter events, 4.5 us)
Async XLA Ops:
  85.4 160.4 %all-to-all-start = ((bf16[1,3,256,4096]{2,1,0,3:T(4,128)(2,1)}), bf16[1,3,256,4096]{2,1,0,3:T(4,128)(2,1)}, u32[]{:S(2)}, u32[]{:S(2)}) async-start(bf16[1,3,256,4096]{2,1,0,3:T(4,128)(2,1)} %copy.22), calls=%async_computation | async-start | bytes 16777216 | tf_op jit(solution)/shard_map/all_to_all | solution.py:360
  245.8 187.3 %all-to-all-start.1 = ((bf16[1,3,256,4096]{2,1,0,3:T(4,128)(2,1)}), bf16[1,3,256,4096]{2,1,0,3:T(4,128)(2,1)}, u32[]{:S(2)}, u32[]{:S(2)}) async-start(bf16[1,3,256,4096]{2,1,0,3:T(4,128)(2,1)} %copy.25), calls=%async_computation.1 | async-start | bytes 16777216 | tf_op jit(solution)/shard_map/all_to_all | solution.py:360
  465.4 0.7 copy-start

commit v2 on v0

--- a/solution.py
+++ b/solution.py
@@ -1,6 +1,10 @@
+import functools
+
 import jax
 import jax.numpy as jnp
 from jax import lax
+from jax.experimental import pallas as pl
+from jax.experimental.pallas import tpu as pltpu
 from jax.sharding import PartitionSpec as P
 
 BS = 64
@@ -8,6 +12,7 @@
 HG = 1
 KN = 3
 KG = 3
+MESH = pl.DeviceIdType.MESH
 
 
 def invert(block_of_slot):
@@ -87,9 +92,287 @@
     )
 
 
+def row_sliced(shape):
+    n = shape["pair"]
+    return shape["grp"] == 2 and BS % n == 0 and (BS // n) * BS % 128 == 0
+
+
+def greet(n, me):
+    barrier = pltpu.get_barrier_semaphore()
+
+    def hello(k, carry):
+        pl.semaphore_signal(
+            barrier, inc=1, device_id={"pair": lax.rem(me + k, n)}, device_id_type=MESH
+        )
+        return carry
+
+    lax.fori_loop(1, n, hello, 0)
+    pl.semaphore_signal(
+        barrier, inc=1, device_id={"grp": 1 - lax.axis_index("grp")}, device_id_type=MESH
+    )
+    pl.semaphore_wait(barrier, n)
+
+
+def swap_major(chunks):
+    return jnp.swapaxes(jnp.stack(chunks, axis=0), 0, 1)
+
+
+def left_chunk(green_ref, tensor_ref, left_ref, rows_at, count):
+    half = count // 2
+    pairs = BS * BS // 128
+    at = pl.ds(rows_at, count)
+    low = lax.broadcasted_iota(jnp.int32, (half, pairs, 128), 2) < BS
+    rows = []
+    for a in range(KN):
+        x = swap_major([tensor_ref[0, a, at, 128 * t : 128 * (t + 1)] for t in range(pairs)])
+        first, second = x[:half], x[half:]
+        even = jnp.where(low, first, pltpu.roll(second, BS, 2))
+        odd = jnp.where(low, pltpu.roll(first, BS, 2), second)
+        for y in (even, odd):
+            rows.append(jnp.concatenate([y[p] for p in range(half)], axis=1))
+    stacked = jnp.concatenate(rows, axis=0)
+    result = jnp.dot(green_ref[...], stacked, preferred_element_type=jnp.float32)
+    result = result.astype(jnp.bfloat16)
+    for a in range(KN):
+        base = a * BS
+        even = jnp.stack(
+            [result[base : base + pairs, 128 * p : 128 * (p + 1)] for p in range(half)], axis=0
+        )
+        odd = jnp.stack(
+            [result[base + pairs : base + BS, 128 * p : 128 * (p + 1)] for p in range(half)],
+            axis=0,
+        )
+        first = jnp.where(low, even, pltpu.roll(odd, BS, 2))
+        second = jnp.where(low, pltpu.roll(even, BS, 2), odd)
+        back = jnp.swapaxes(jnp.concatenate([first, second], axis=0), 0, 1)
+        for t in range(pairs):
+            left_ref[a, at, 128 * t : 128 * (t + 1)] = back[t]
+
+
+def fill_green(n, column, slots_ref, pack_ref, every_ref, green_ref):
+    keep_row = KG * BS
+    for target in range(-HB, HB + 1):
+        line = []
+        for source in range(-HB, HB + 1):
+            step = target - source
+            if abs(step) <= HG:
+                slot = slots_ref[lax.rem(column + source + n, n)]
+                at = (step + HG) * BS
+                block = every_ref[slot, at : at + BS, :][:, :BS].astype(jnp.float32)
+                keep = pack_ref[keep_row : keep_row + 16, :][:1, source + HB : source + HB + 1]
+                line.append((block * keep.astype(jnp.float32)).astype(jnp.bfloat16))
+            else:
+                line.append(jnp.zeros((BS, BS), jnp.bfloat16))
+        at = (target + HB) * BS
+        green_ref[at : at + BS, :] = jnp.concatenate(line, axis=1)
+
+
+def chi_of_block(n, lam, slots_ref, every_ref, left_rows, tensor_rows, part_ref):
+    aux, width = tensor_rows.shape[2:]
+    rows = width // BS
+    here = slots_ref[lam]
+    line = lax.broadcasted_iota(jnp.int32, (width, width), 0) // BS
+    column = lax.broadcasted_iota(jnp.int32, (width, width), 1) // BS
+    spread = []
+    for c in range(KG):
+        block = every_ref[here, c * BS : (c + 1) * BS, :][:, BS : 2 * BS]
+        block = jnp.concatenate([block] * rows, axis=1)
+        block = jnp.concatenate([block] * rows, axis=0)
+        spread.append(jnp.where(line == column, block, jnp.zeros_like(block)))
+    keeps = every_ref[here, KG * BS : KG * BS + 16, :][:1].astype(jnp.float32)
+    total = part_ref[...]
+    for a in range(-HB, HB + 1):
+        right = jnp.zeros((aux, width), jnp.float32)
+        for c in range(-HG, HG + 1):
+            if abs(a - c) <= HB:
+                slot = slots_ref[lax.rem(lam + c + n, n)]
+                right = right + jnp.dot(
+                    left_rows[slot, a - c + HB],
+                    spread[c + HG],
+                    preferred_element_type=jnp.float32,
+                )
+        right = (right * keeps[:, a + HB : a + HB + 1]).astype(jnp.bfloat16)
+        total = total + lax.dot_general(
+            tensor_rows[here, a + HB],
+            right,
+            (((1,), (1,)), ((), ())),
+            preferred_element_type=jnp.float32,
+        )
+    part_ref[...] = total
+
+
+def whole_kernel(
+    n, chunk, blocks_ref, slots_ref, pack_ref, tensor_ref, out_ref,
+    every, green, left, left_rows, tensor_rows, part, landed,
+    pack_send, pack_recv, tensor_send, tensor_recv, pass_send, pass_recv,
+    left_send, left_recv, chi_send, chi_recv, own_sem,
+):
+    me = lax.axis_index("pair")
+    grp = lax.axis_index("grp")
+    aux = tensor_ref.shape[2]
+    width = tensor_rows.shape[3]
+    chunks = aux // chunk
+    out_rows = aux // n
+    share = pl.ds(pl.multiple_of(grp * (aux // 2), aux // 2), aux // 2)
+    mine = pl.ds(pl.multiple_of(me * width, width), width)
+
+    def lanes(to):
+        return pl.ds(pl.multiple_of(to * width, width), width)
+
+    def remote(src, dst, send, recv, target):
+        return pltpu.make_async_remote_copy(
+            src_ref=src, dst_ref=dst, send_sem=send, recv_sem=recv,
+            device_id=target, device_id_type=MESH,
+        )
+
+    def pack_copy(k):
+        to = lax.rem(me + k, n)
+        return remote(pack_ref, every.at[me], pack_send.at[k], pack_recv.at[k], {"pair": to})
+
+    def tensor_copy(k):
+        to = lax.rem(me + k, n)
+        return remote(
+            tensor_ref.at[0, :, share, lanes(to)], tensor_rows.at[me, :, share, :],
+            tensor_send.at[k], tensor_recv.at[k], {"pair": to},
+        )
+
+    def pass_copy(k):
+        source = lax.rem(me - k + n, n)
+        where = tensor_rows.at[source, :, share, :]
+        return remote(where, where, pass_send.at[k], pass_recv.at[k], {"grp": 1 - grp})
+
+    def left_copy(q, k):
+        to = lax.rem(me + k, n)
+        at = pl.ds(pl.multiple_of(q * chunk, chunk), chunk)
+        return remote(
+            left.at[:, at, lanes(to)], left_rows.at[me, :, at, :],
+            left_send.at[q, k], left_recv.at[q, k], {"pair": to},
+        )
+
+    def chi_copy(k):
+        to = lax.rem(me + k, n)
+        return remote(
+            part.at[pl.ds(pl.multiple_of(to * out_rows, out_rows), out_rows)], landed.at[k],
+            chi_send.at[k], chi_recv.at[k], {"pair": to},
+        )
+
+    def each(act, low=1):
+        def body(k, carry):
+            act(k)
+            return carry
+
+        lax.fori_loop(low, n, body, 0)
+
+    greet(n, me)
+    each(lambda k: pack_copy(k).start())
+    each(lambda k: tensor_copy(k).start())
+    own_pack = pltpu.make_async_copy(pack_ref, every.at[me], own_sem.at[0])
+    own_tensor = pltpu.make_async_copy(
+        tensor_ref.at[0, :, :, mine], tensor_rows.at[me], own_sem.at[1]
+    )
+    own_pack.start()
+    own_tensor.start()
+    own_pack.wait()
+    each(lambda k: pack_copy(k).wait_recv())
+    fill_green(n, blocks_ref[me], slots_ref, pack_ref, every, green)
+
+    def make_left(q, carry):
+        left_chunk(green, tensor_ref, left, pl.multiple_of(q * chunk, chunk), chunk)
+        each(lambda k: left_copy(q, k).start())
+        return carry
+
+    lax.fori_loop(0, chunks, make_left, 0)
+    own_left = pltpu.make_async_copy(left.at[:, :, mine], left_rows.at[me], own_sem.at[2])
+    own_left.start()
+
+    def hand_on(k):
+        tensor_copy(k).wait_recv()
+        pass_copy(k).start()
+
+    each(hand_on)
+    part[...] = jnp.zeros_like(part)
+    own_tensor.wait()
+    own_left.wait()
+
+    def left_all(k):
+        def body(q, carry):
+            left_copy(q, k).wait_recv()
+            return carry
+
+        lax.fori_loop(0, chunks, body, 0)
+
+    each(lambda k: pass_copy(k).wait_recv())
+    each(left_all)
+
+    def add_block(lam, carry):
+        chi_of_block(n, lam, slots_ref, every, left_rows, tensor_rows, part)
+        return carry
+
+    lax.fori_loop(0, n, add_block, 0)
+    each(lambda k: chi_copy(k).start())
+
+    def sent(k):
+        pack_copy(k).wait_send()
+        tensor_copy(k).wait_send()
+        pass_copy(k).wait_send()
+
+        def body(q, carry):
+            left_copy(q, k).wait_send()
+            return carry
+
+        lax.fori_loop(0, chunks, body, 0)
+
+    each(sent)
+    each(lambda k: chi_copy(k).wait_recv())
+    total = part[pl.ds(pl.multiple_of(me * out_rows, out_rows), out_rows), :]
+    for k in range(1, n):
+        total = total + landed[k]
+    out_ref[...] = total
+    each(lambda k: chi_copy(k).wait_send())
+
+
+def by_row_slices(three_center, block_mask, green_occ, green_virt, green_mask, block_of_slot):
+    n = lax.axis_size("pair")
+    aux = three_center.shape[2]
+    width = BS * BS // n
+    chunk = 32
+    slot_of_block = invert(block_of_slot)
+    keep = green_mask.astype(jnp.bfloat16)[0, :, None, None]
+    occ = green_occ.reshape(KG, BS // 2, 2, BS // 2, 2).transpose(0, 2, 1, 4, 3)
+    occ = occ.reshape(KG, BS, BS)
+    virt = green_virt.reshape(KG, BS, BS)
+    greens = (jnp.concatenate([occ, virt], axis=2) * keep).reshape(KG * BS, 2 * BS)
+    mask = jnp.pad(block_mask.astype(jnp.bfloat16), ((0, 15), (0, 2 * BS - KN)))
+    pack = jnp.concatenate([greens, mask], axis=0)
+    smem = pl.BlockSpec(memory_space=pltpu.SMEM)
+    vmem = pl.BlockSpec(memory_space=pltpu.VMEM)
+    sems = pltpu.SemaphoreType.DMA
+    return pl.pallas_call(
+        functools.partial(whole_kernel, n, chunk),
+        out_shape=jax.ShapeDtypeStruct((aux // n, aux), jnp.float32),
+        in_specs=[smem, smem, vmem, vmem],
+        out_specs=vmem,
+        scratch_shapes=[
+            pltpu.VMEM((n,) + pack.shape, jnp.bfloat16),
+            pltpu.VMEM((KN * BS, KN * BS), jnp.bfloat16),
+            pltpu.VMEM((KN, aux, BS * BS), jnp.bfloat16),
+            pltpu.VMEM((n, KN, aux, width), jnp.bfloat16),
+            pltpu.VMEM((n, KN, aux, width), jnp.bfloat16),
+            pltpu.VMEM((aux, aux), jnp.float32),
+            pltpu.VMEM((n, aux // n, aux), jnp.float32),
+            sems((n,)), sems((n,)), sems((n,)), sems((n,)), sems((n,)), sems((n,)),
+            sems((aux // chunk, n)), sems((aux // chunk, n)), sems((n,)), sems((n,)), sems((3,)),
+        ],
+        compiler_params=pltpu.CompilerParams(
+            collective_id=0, has_side_effects=True, vmem_limit_bytes=48 * 1024 * 1024
+        ),
+        name="polarizability",
+    )(block_of_slot, slot_of_block, pack, three_center)
+
+
 def solution(mesh):
     return jax.shard_map(
-        on_device,
+        by_row_slices if row_sliced(mesh.shape) else on_device,
         mesh=mesh,
         in_specs=(
             P("pair", None, None, None),

time: 709 us -> 265 us (0.37); the launches traced: 697 us -> 265 us
  Pallas kernels: 0 us -> 254 us
  blocking collectives: 215 us -> 0 us
  local copies, waits for them, and re-layouts: 206 us -> 8.57 us
  waiting for transfers between devices: 181 us -> 0 us
  other arithmetic: 45.6 us -> 2.1 us
  matrix products: 23.3 us -> 0 us
  between operations: 13.9 us -> 0.06 us
  starting transfers between devices: 12.4 us -> 0 us
    pallas_call x0 -> x1, Pallas kernels: none -> 254 us  [by_row_slices(): pl.pallas_call(functools.partial(whole_kernel, n, chunk), out_shape=jax.S...]
    all_gather x2 -> x0, blocking collectives: 215 us -> none  [the longest x1 167 us: on_device(): lax.all_gather(green_virt * green_keep, 'pair', axis=0, tiled=True)]
    all_to_all x2 -> x0, waiting for transfers between devices: 102 us -> none  [the longest x1 102 us: on_device(): lax.all_to_all(right_slots, 'pair', split_axis=0, concat_axis=2, tiled=True)]
    reduce_scatter x1 -> x0, waiting for transfers between devices: 78.8 us -> none  [on_device(): lax.psum_scatter(lax.dot_general(masked, returned, (((0, 1, 3), (0, 1, 3)...]
    reshape x8 -> x1, local copies, waits for them, and re-layouts: 73 us -> 4.17 us  [by_row_slices(): occ = green_occ.reshape(KG, BS // 2, 2, BS // 2, 2).transpose(0, 2, 1, 4, 3)]
    another operation x8 -> x0, local copies, waits for them, and re-layouts: 40.8 us -> none  [the longest x1 17.2 us: build_left(): tensor_cat.reshape(blocks.shape[0], len(middles) * BS, blocks.shape[3])]
    transpose x2 -> x0, local copies, waits for them, and re-layouts: 37.3 us -> none  [the longest x1 21.8 us: on_device(): left.transpose(0, 1, 4, 3, 2).reshape(block_count, KN, BS, local_aux * BS)]
    dot_general x7 -> x0, matrix products: 23.3 us -> none  [the longest x1 8.16 us: on_device(): lax.dot_general(masked, returned, (((0, 1, 3), (0, 1, 3)), ((), ())), pre...]
  transfers between devices with their start and end apart: 3 -> 0, of which waited for: 2 -> 0; matrix products, arithmetic and copies ran while one was open for 4% -> 0% of each run, Pallas kernels for 0% -> 0%
where the time goes in v2:
time: 265 us
  Pallas kernels  254 us (96%)
  local copies, waits for them, and re-layouts  8.57 us (3%)
    pallas_call x1, Pallas kernels, by_row_slices(): pl.pallas_call(functools.partial(whole_kernel, n, chunk), out_shape=jax.S...  254 us

profile of v2, /device:TPU:0, one launch (start us, length us, event | category | flops | bytes accessed | tf_op | source)
XLA Modules:
  0.0 264.8 jit_solution(181238361910556883)
XLA Ops:
  0.0 4.2 %reshape.12 = bf16[3,32,2,32,2]{4,3,2,1,0:T(8,128)(2,1)S(1)} reshape(bf16[1,3,4096]{2,1,0:T(4,128)(2,1)} %param.8) | data formatting | bytes 49152 | tf_op jit(solution)/shard_map/reshape | solution.py:341
  4.2 1.4 copy.10
  5.6 0.1 reshape.22
  5.7 0.9 concatenate.12
  6.6 0.7 convert_bitcast_fusion
  7.2 0.1 mul.16
  7.3 0.1 mul.17
  7.4 0.1 maximum_multiply_fusion
  7.5 0.7 convert_element_type.9
  8.2 0.7 compare_select_fusion
  8.8 0.6 scatter_custom_fusion.slots_ref
  9.4 0.0 copy-start
  9.5 0.6 copy-done
  10.1 254.1 %polarizability.1 = f32[16,256]{1,0:T(8,128)S(1)} custom-call(s32[16]{0:T(128)S(1)} %copy-done, s32[16]{0:T(128)S(1)} %scatter_custom_fusion.slots_ref, bf16[208,128]{1,0:T(8,128)(2,1)S(1)} %fusion.1.pack_ref, bf16[1,3,256,4096]{3,2,1,0:T(8,128)(2,1)} %tensor_ref.1), custom_call_target="tpu_custom_call" | custom-call | tf_op jit(solution)/shard_map/polarizability/pallas_call | solution.py:350
  264.2 0.6 copy.13
  (2 shorter events, 0.0 us)
Async XLA Ops:
  9.4 0.7 copy-start

commit v3 on v2

--- a/solution.py
+++ b/solution.py
@@ -124,7 +124,7 @@
     low = lax.broadcasted_iota(jnp.int32, (half, pairs, 128), 2) < BS
     rows = []
     for a in range(KN):
-        x = swap_major([tensor_ref[0, a, at, 128 * t : 128 * (t + 1)] for t in range(pairs)])
+        x = swap_major([tensor_ref[a, at, 128 * t : 128 * (t + 1)] for t in range(pairs)])
         first, second = x[:half], x[half:]
         even = jnp.where(low, first, pltpu.roll(second, BS, 2))
         odd = jnp.where(low, pltpu.roll(first, BS, 2), second)
@@ -149,8 +149,10 @@
             left_ref[a, at, 128 * t : 128 * (t + 1)] = back[t]
 
 
-def fill_green(n, column, slots_ref, pack_ref, every_ref, green_ref):
+def fill_green(n, column, slots_ref, every_ref, green_ref):
     keep_row = KG * BS
+    own = slots_ref[column]
+    keeps = every_ref[own, keep_row : keep_row + 16, :][:1].astype(jnp.float32)
     for target in range(-HB, HB + 1):
         line = []
         for source in range(-HB, HB + 1):
@@ -159,53 +161,54 @@
                 slot = slots_ref[lax.rem(column + source + n, n)]
                 at = (step + HG) * BS
                 block = every_ref[slot, at : at + BS, :][:, :BS].astype(jnp.float32)
-                keep = pack_ref[keep_row : keep_row + 16, :][:1, source + HB : source + HB + 1]
-                line.append((block * keep.astype(jnp.float32)).astype(jnp.bfloat16))
+                keep = keeps[:, source + HB : source + HB + 1]
+                line.append((block * keep).astype(jnp.bfloat16))
             else:
                 line.append(jnp.zeros((BS, BS), jnp.bfloat16))
         at = (target + HB) * BS
         green_ref[at : at + BS, :] = jnp.concatenate(line, axis=1)
 
 
-def chi_of_block(n, lam, slots_ref, every_ref, left_rows, tensor_rows, part_ref):
-    aux, width = tensor_rows.shape[2:]
+def fill_virt(slot, c, every_ref, virt_ref, which):
+    width = virt_ref.shape[1]
     rows = width // BS
-    here = slots_ref[lam]
     line = lax.broadcasted_iota(jnp.int32, (width, width), 0) // BS
     column = lax.broadcasted_iota(jnp.int32, (width, width), 1) // BS
-    spread = []
-    for c in range(KG):
-        block = every_ref[here, c * BS : (c + 1) * BS, :][:, BS : 2 * BS]
-        block = jnp.concatenate([block] * rows, axis=1)
-        block = jnp.concatenate([block] * rows, axis=0)
-        spread.append(jnp.where(line == column, block, jnp.zeros_like(block)))
-    keeps = every_ref[here, KG * BS : KG * BS + 16, :][:1].astype(jnp.float32)
-    total = part_ref[...]
+    at = (c + HG) * BS
+    block = every_ref[slot, at : at + BS, :][:, BS : 2 * BS]
+    block = jnp.concatenate([block] * rows, axis=1)
+    block = jnp.concatenate([block] * rows, axis=0)
+    virt_ref[which] = jnp.where(line == column, block, jnp.zeros_like(block))
+
+
+def add_lanes(at, keeps, here, after, left, left_after, virt, part):
+    def times(value, which):
+        return jnp.dot(value, virt[which], preferred_element_type=jnp.float32)
+
+    def against(tensor, right):
+        return lax.dot_general(
+            tensor, right, (((1,), (1,)), ((), ())), preferred_element_type=jnp.float32
+        )
+
+    total = part[...]
     for a in range(-HB, HB + 1):
-        right = jnp.zeros((aux, width), jnp.float32)
-        for c in range(-HG, HG + 1):
-            if abs(a - c) <= HB:
-                slot = slots_ref[lax.rem(lam + c + n, n)]
-                right = right + jnp.dot(
-                    left_rows[slot, a - c + HB],
-                    spread[c + HG],
-                    preferred_element_type=jnp.float32,
-                )
-        right = (right * keeps[:, a + HB : a + HB + 1]).astype(jnp.bfloat16)
-        total = total + lax.dot_general(
-            tensor_rows[here, a + HB],
-            right,
-            (((1,), (1,)), ((), ())),
-            preferred_element_type=jnp.float32,
-        )
-    part_ref[...] = total
+        mid = left[a + HB, :, at]
+        right = times(mid, 0)
+        if a >= 0:
+            right = right + times(left_after[a - 1 + HB, :, at], 1)
+        right = (right * keeps[0][:, a + HB : a + HB + 1]).astype(jnp.bfloat16)
+        total = total + against(here[a + HB, :, at], right)
+        if a >= 0:
+            right = times(mid, 2) * keeps[1][:, a - 1 + HB : a + HB]
+            total = total + against(after[a - 1 + HB, :, at], right.astype(jnp.bfloat16))
+    part[...] = total
 
 
 def whole_kernel(
     n, chunk, blocks_ref, slots_ref, pack_ref, tensor_ref, out_ref,
-    every, green, left, left_rows, tensor_rows, part, landed,
-    pack_send, pack_recv, tensor_send, tensor_recv, pass_send, pass_recv,
-    left_send, left_recv, chi_send, chi_recv, own_sem,
+    every, green, green_after, virt, left, left_after, rolled, tensor_rows, staged, part, landed,
+    pack_send, pack_recv, tensor_send, tensor_recv, back_send, back_recv, pass_send, pass_recv,
+    chi_send, chi_recv, own_sem,
 ):
     me = lax.axis_index("pair")
     grp = lax.axis_index("grp")
@@ -213,8 +216,8 @@
     width = tensor_rows.shape[3]
     chunks = aux // chunk
     out_rows = aux // n
-    share = pl.ds(pl.multiple_of(grp * (aux // 2), aux // 2), aux // 2)
-    mine = pl.ds(pl.multiple_of(me * width, width), width)
+    half = aux // 2
+    share = pl.ds(pl.multiple_of(grp * half, half), half)
 
     def lanes(to):
         return pl.ds(pl.multiple_of(to * width, width), width)
@@ -232,22 +235,20 @@
     def tensor_copy(k):
         to = lax.rem(me + k, n)
         return remote(
-            tensor_ref.at[0, :, share, lanes(to)], tensor_rows.at[me, :, share, :],
+            tensor_ref.at[0, :, share, lanes(to)], tensor_rows.at[me],
             tensor_send.at[k], tensor_recv.at[k], {"pair": to},
         )
 
+    def back_copy(k):
+        to = lax.rem(me + k, n)
+        return remote(
+            staged.at[to], rolled.at[:, share, lanes(me)],
+            back_send.at[k], back_recv.at[k], {"pair": to},
+        )
+
     def pass_copy(k):
-        source = lax.rem(me - k + n, n)
-        where = tensor_rows.at[source, :, share, :]
+        where = rolled.at[:, share, lanes(lax.rem(me - k + n, n))]
         return remote(where, where, pass_send.at[k], pass_recv.at[k], {"grp": 1 - grp})
-
-    def left_copy(q, k):
-        to = lax.rem(me + k, n)
-        at = pl.ds(pl.multiple_of(q * chunk, chunk), chunk)
-        return remote(
-            left.at[:, at, lanes(to)], left_rows.at[me, :, at, :],
-            left_send.at[q, k], left_recv.at[q, k], {"pair": to},
-        )
 
     def chi_copy(k):
         to = lax.rem(me + k, n)
@@ -256,73 +257,94 @@
             chi_send.at[k], chi_recv.at[k], {"pair": to},
         )
 
-    def each(act, low=1):
+    def each(act, low=1, high=n):
         def body(k, carry):
             act(k)
             return carry
 
-        lax.fori_loop(low, n, body, 0)
+        lax.fori_loop(low, high, body, 0)
 
     greet(n, me)
     each(lambda k: pack_copy(k).start())
     each(lambda k: tensor_copy(k).start())
     own_pack = pltpu.make_async_copy(pack_ref, every.at[me], own_sem.at[0])
     own_tensor = pltpu.make_async_copy(
-        tensor_ref.at[0, :, :, mine], tensor_rows.at[me], own_sem.at[1]
+        tensor_ref.at[0, :, share, lanes(me)], tensor_rows.at[me], own_sem.at[1]
     )
     own_pack.start()
     own_tensor.start()
     own_pack.wait()
     each(lambda k: pack_copy(k).wait_recv())
-    fill_green(n, blocks_ref[me], slots_ref, pack_ref, every, green)
-
-    def make_left(q, carry):
-        left_chunk(green, tensor_ref, left, pl.multiple_of(q * chunk, chunk), chunk)
-        each(lambda k: left_copy(q, k).start())
-        return carry
-
-    lax.fori_loop(0, chunks, make_left, 0)
-    own_left = pltpu.make_async_copy(left.at[:, :, mine], left_rows.at[me], own_sem.at[2])
-    own_left.start()
+    column = blocks_ref[me]
+    column_after = lax.rem(column + 1, n)
+    slot, slot_after = slots_ref[column], slots_ref[column_after]
+    fill_green(n, column, slots_ref, every, green)
+    fill_green(n, column_after, slots_ref, every, green_after)
+    fill_virt(slot, 0, every, virt, 0)
+    fill_virt(slot, 1, every, virt, 1)
+    fill_virt(slot_after, -1, every, virt, 2)
+
+    def own_left(q):
+        left_chunk(green, tensor_ref.at[0], left, pl.multiple_of(q * chunk, chunk), chunk)
+
+    each(own_left, 0, chunks)
+    own_tensor.wait()
+    each(lambda k: tensor_copy(k).wait_recv())
+
+    def stage(k):
+        to = lax.rem(me + k, n)
+        wanted = slots_ref[lax.rem(blocks_ref[to] + 1, n)]
+        for a in range(KN):
+            staged[to, a] = tensor_rows[wanted, a]
+
+    def stage_and_send(k):
+        stage(k)
+        back_copy(k).start()
+
+    each(stage_and_send)
+    stage(0)
+    own_back = pltpu.make_async_copy(
+        staged.at[me], rolled.at[:, share, lanes(me)], own_sem.at[2]
+    )
+    own_back.start()
+    own_back.wait()
+    pass_copy(0).start()
 
     def hand_on(k):
-        tensor_copy(k).wait_recv()
+        back_copy(k).wait_recv()
         pass_copy(k).start()
 
     each(hand_on)
+
+    def after_left(base):
+        def act(q):
+            at = pl.multiple_of(base + q * chunk, chunk)
+            left_chunk(green_after, rolled, left_after, at, chunk)
+
+        each(act, 0, chunks // 2)
+
+    after_left(grp * half)
+    each(lambda k: pass_copy(k).wait_recv(), 0)
+    after_left((1 - grp) * half)
     part[...] = jnp.zeros_like(part)
-    own_tensor.wait()
-    own_left.wait()
-
-    def left_all(k):
-        def body(q, carry):
-            left_copy(q, k).wait_recv()
-            return carry
-
-        lax.fori_loop(0, chunks, body, 0)
-
-    each(lambda k: pass_copy(k).wait_recv())
-    each(left_all)
-
-    def add_block(lam, carry):
-        chi_of_block(n, lam, slots_ref, every, left_rows, tensor_rows, part)
-        return carry
-
-    lax.fori_loop(0, n, add_block, 0)
+    keeps = [
+        every[s, KG * BS : KG * BS + 16, :][:1].astype(jnp.float32) for s in (slot, slot_after)
+    ]
+
+    def add(t):
+        at = pl.ds(pl.multiple_of(t * virt.shape[1], virt.shape[1]), virt.shape[1])
+        add_lanes(at, keeps, tensor_ref.at[0], rolled, left, left_after, virt, part)
+
+    each(add, 0, left.shape[2] // virt.shape[1])
     each(lambda k: chi_copy(k).start())
 
     def sent(k):
         pack_copy(k).wait_send()
         tensor_copy(k).wait_send()
-        pass_copy(k).wait_send()
-
-        def body(q, carry):
-            left_copy(q, k).wait_send()
-            return carry
-
-        lax.fori_loop(0, chunks, body, 0)
+        back_copy(k).wait_send()
 
     each(sent)
+    each(lambda k: pass_copy(k).wait_send(), 0)
     each(lambda k: chi_copy(k).wait_recv())
     total = part[pl.ds(pl.multiple_of(me * out_rows, out_rows), out_rows), :]
     for k in range(1, n):
@@ -355,13 +377,19 @@
         scratch_shapes=[
             pltpu.VMEM((n,) + pack.shape, jnp.bfloat16),
             pltpu.VMEM((KN * BS, KN * BS), jnp.bfloat16),
+            pltpu.VMEM((KN * BS, KN * BS), jnp.bfloat16),
+            pltpu.VMEM((3, 4 * BS, 4 * BS), jnp.bfloat16),
             pltpu.VMEM((KN, aux, BS * BS), jnp.bfloat16),
-            pltpu.VMEM((n, KN, aux, width), jnp.bfloat16),
-            pltpu.VMEM((n, KN, aux, width), jnp.bfloat16),
+            pltpu.VMEM((KN, aux, BS * BS), jnp.bfloat16),
+            pltpu.VMEM((KN, aux, BS * BS), jnp.bfloat16),
+            pltpu.VMEM((n, KN, aux // 2, width), jnp.bfloat16),
+            pltpu.VMEM((n, KN, aux // 2, width), jnp.bfloat16),
             pltpu.VMEM((aux, aux), jnp.float32),
             pltpu.VMEM((n, aux // n, aux), jnp.float32),
-            sems((n,)), sems((n,)), sems((n,)), sems((n,)), sems((n,)), sems((n,)),
-            sems((aux // chunk, n)), sems((aux // chunk, n)), sems((n,)), sems((n,)), sems((3,)),
+        ]
+        + [sems((n,))] * 10
+        + [
+            sems((3,)),
         ],
         compiler_params=pltpu.CompilerParams(
             collective_id=0, has_side_effects=True, vmem_limit_bytes=48 * 1024 * 1024

time: 265 us -> 240 us (0.906)
  Pallas kernels: 254 us -> 227 us
    pallas_call x1, Pallas kernels: 254 us -> 227 us  [by_row_slices(): pl.pallas_call(functools.partial(whole_kernel, n, chunk), out_shape=jax.S...]
where the time goes in v3:
time: 240 us; the launch traced here: 238 us
  Pallas kernels  227 us (95%)
  local copies, waits for them, and re-layouts  8.57 us (4%)
    pallas_call x1, Pallas kernels, by_row_slices(): pl.pallas_call(functools.partial(whole_kernel, n, chunk), out_shape=jax.S...  227 us

profile of v3, /device:TPU:0, one launch (start us, length us, event | category | flops | bytes accessed | tf_op | source)
XLA Modules:
  0.0 238.1 jit_solution(7470148816715677880)
XLA Ops:
  0.0 4.2 %reshape.12 = bf16[3,32,2,32,2]{4,3,2,1,0:T(8,128)(2,1)S(1)} reshape(bf16[1,3,4096]{2,1,0:T(4,128)(2,1)} %param.8) | data formatting | bytes 49152 | tf_op jit(solution)/shard_map/reshape | solution.py:363
  4.2 1.4 copy.10
  5.6 0.1 reshape.22
  5.7 0.9 concatenate.12
  6.6 0.7 convert_bitcast_fusion
  7.2 0.1 mul.16
  7.3 0.1 mul.17
  7.4 0.1 maximum_multiply_fusion
  7.5 0.7 convert_element_type.9
  8.2 0.7 compare_select_fusion
  8.8 0.6 scatter_custom_fusion.slots_ref
  9.4 0.0 copy-start
  9.5 0.6 copy-done
  10.1 227.3 %polarizability.1 = f32[16,256]{1,0:T(8,128)S(1)} custom-call(s32[16]{0:T(128)S(1)} %copy-done, s32[16]{0:T(128)S(1)} %scatter_custom_fusion.slots_ref, bf16[208,128]{1,0:T(8,128)(2,1)S(1)} %fusion.1.pack_ref, bf16[1,3,256,4096]{3,2,1,0:T(8,128)(2,1)} %tensor_ref.1), custom_call_target="tpu_custom_call" | custom-call | tf_op jit(solution)/shard_map/polarizability/pallas_call | solution.py:372
  237.5 0.6 copy.13
  (2 shorter events, 0.0 us)
Async XLA Ops:
  9.4 0.7 copy-start

commit v4 on v3

--- a/solution.py
+++ b/solution.py
@@ -206,18 +206,23 @@
 
 def whole_kernel(
     n, chunk, blocks_ref, slots_ref, pack_ref, tensor_ref, out_ref,
-    every, green, green_after, virt, left, left_after, rolled, tensor_rows, staged, part, landed,
+    every, green, green_after, virt, left, left_after, rolled, part, landed,
     pack_send, pack_recv, tensor_send, tensor_recv, back_send, back_recv, pass_send, pass_recv,
-    chi_send, chi_recv, own_sem,
+    chi_send, chi_recv, own_sem, own_tensor_sem, own_back_sem, *buffers,
 ):
     me = lax.axis_index("pair")
     grp = lax.axis_index("grp")
     aux = tensor_ref.shape[2]
-    width = tensor_rows.shape[3]
+    pieces = len(buffers) // 2
+    tensor_rows, staged = buffers[:pieces], buffers[pieces:]
+    piece = aux // 2 // pieces
+    width = tensor_rows[0].shape[3]
     chunks = aux // chunk
     out_rows = aux // n
     half = aux // 2
-    share = pl.ds(pl.multiple_of(grp * half, half), half)
+
+    def share(p):
+        return pl.ds(pl.multiple_of(grp * half + p * piece, piece), piece)
 
     def lanes(to):
         return pl.ds(pl.multiple_of(to * width, width), width)
@@ -232,23 +237,23 @@
         to = lax.rem(me + k, n)
         return remote(pack_ref, every.at[me], pack_send.at[k], pack_recv.at[k], {"pair": to})
 
-    def tensor_copy(k):
+    def tensor_copy(p, k):
         to = lax.rem(me + k, n)
         return remote(
-            tensor_ref.at[0, :, share, lanes(to)], tensor_rows.at[me],
-            tensor_send.at[k], tensor_recv.at[k], {"pair": to},
-        )
-
-    def back_copy(k):
+            tensor_ref.at[0, :, share(p), lanes(to)], tensor_rows[p].at[me],
+            tensor_send.at[p, k], tensor_recv.at[p, k], {"pair": to},
+        )
+
+    def back_copy(p, k):
         to = lax.rem(me + k, n)
         return remote(
-            staged.at[to], rolled.at[:, share, lanes(me)],
-            back_send.at[k], back_recv.at[k], {"pair": to},
-        )
-
-    def pass_copy(k):
-        where = rolled.at[:, share, lanes(lax.rem(me - k + n, n))]
-        return remote(where, where, pass_send.at[k], pass_recv.at[k], {"grp": 1 - grp})
+            staged[p].at[to], rolled.at[:, share(p), lanes(me)],
+            back_send.at[p, k], back_recv.at[p, k], {"pair": to},
+        )
+
+    def pass_copy(p, k):
+        where = rolled.at[:, share(p), lanes(lax.rem(me - k + n, n))]
+        return remote(where, where, pass_send.at[p, k], pass_recv.at[p, k], {"grp": 1 - grp})
 
     def chi_copy(k):
         to = lax.rem(me + k, n)
@@ -264,15 +269,47 @@
 
         lax.fori_loop(low, high, body, 0)
 
+    def own_tensor(p):
+        return pltpu.make_async_copy(
+            tensor_ref.at[0, :, share(p), lanes(me)], tensor_rows[p].at[me], own_tensor_sem.at[p]
+        )
+
+    def own_back(p):
+        return pltpu.make_async_copy(
+            staged[p].at[me], rolled.at[:, share(p), lanes(me)], own_back_sem.at[p]
+        )
+
+    def stage(p, k):
+        to = lax.rem(me + k, n)
+        wanted = slots_ref[lax.rem(blocks_ref[to] + 1, n)]
+        for a in range(KN):
+            staged[p][to, a] = tensor_rows[p][wanted, a]
+
+    def stage_and_send(p, k):
+        stage(p, k)
+        back_copy(p, k).start()
+
+    def own_left(q):
+        left_chunk(green, tensor_ref.at[0], left, pl.multiple_of(q * chunk, chunk), chunk)
+
+    def hand_on(p, k):
+        back_copy(p, k).wait_recv()
+        pass_copy(p, k).start()
+
+    def after_left(base):
+        def act(q):
+            at = pl.multiple_of(base + q * chunk, chunk)
+            left_chunk(green_after, rolled, left_after, at, chunk)
+
+        each(act, 0, piece // chunk)
+
     greet(n, me)
     each(lambda k: pack_copy(k).start())
-    each(lambda k: tensor_copy(k).start())
+    for p in range(pieces):
+        each(lambda k: tensor_copy(p, k).start())
+        own_tensor(p).start()
     own_pack = pltpu.make_async_copy(pack_ref, every.at[me], own_sem.at[0])
-    own_tensor = pltpu.make_async_copy(
-        tensor_ref.at[0, :, share, lanes(me)], tensor_rows.at[me], own_sem.at[1]
-    )
     own_pack.start()
-    own_tensor.start()
     own_pack.wait()
     each(lambda k: pack_copy(k).wait_recv())
     column = blocks_ref[me]
@@ -283,49 +320,22 @@
     fill_virt(slot, 0, every, virt, 0)
     fill_virt(slot, 1, every, virt, 1)
     fill_virt(slot_after, -1, every, virt, 2)
-
-    def own_left(q):
-        left_chunk(green, tensor_ref.at[0], left, pl.multiple_of(q * chunk, chunk), chunk)
-
-    each(own_left, 0, chunks)
-    own_tensor.wait()
-    each(lambda k: tensor_copy(k).wait_recv())
-
-    def stage(k):
-        to = lax.rem(me + k, n)
-        wanted = slots_ref[lax.rem(blocks_ref[to] + 1, n)]
-        for a in range(KN):
-            staged[to, a] = tensor_rows[wanted, a]
-
-    def stage_and_send(k):
-        stage(k)
-        back_copy(k).start()
-
-    each(stage_and_send)
-    stage(0)
-    own_back = pltpu.make_async_copy(
-        staged.at[me], rolled.at[:, share, lanes(me)], own_sem.at[2]
-    )
-    own_back.start()
-    own_back.wait()
-    pass_copy(0).start()
-
-    def hand_on(k):
-        back_copy(k).wait_recv()
-        pass_copy(k).start()
-
-    each(hand_on)
-
-    def after_left(base):
-        def act(q):
-            at = pl.multiple_of(base + q * chunk, chunk)
-            left_chunk(green_after, rolled, left_after, at, chunk)
-
-        each(act, 0, chunks // 2)
-
-    after_left(grp * half)
-    each(lambda k: pass_copy(k).wait_recv(), 0)
-    after_left((1 - grp) * half)
+    per_piece = chunks // pieces
+    for p in range(pieces):
+        own_tensor(p).wait()
+        each(lambda k: tensor_copy(p, k).wait_recv())
+        each(lambda k: stage_and_send(p, k))
+        stage(p, 0)
+        own_back(p).start()
+        each(own_left, p * per_piece, (p + 1) * per_piece)
+    for p in range(pieces):
+        own_back(p).wait()
+        pass_copy(p, 0).start()
+        each(lambda k: hand_on(p, k))
+        after_left(grp * half + p * piece)
+    for p in range(pieces):
+        each(lambda k: pass_copy(p, k).wait_recv(), 0)
+        after_left((1 - grp) * half + p * piece)
     part[...] = jnp.zeros_like(part)
     keeps = [
         every[s, KG * BS : KG * BS + 16, :][:1].astype(jnp.float32) for s in (slot, slot_after)
@@ -340,11 +350,13 @@
 
     def sent(k):
         pack_copy(k).wait_send()
-        tensor_copy(k).wait_send()
-        back_copy(k).wait_send()
+        for p in range(pieces):
+            tensor_copy(p, k).wait_send()
+            back_copy(p, k).wait_send()
 
     each(sent)
-    each(lambda k: pass_copy(k).wait_send(), 0)
+    for p in range(pieces):
+        each(lambda k: pass_copy(p, k).wait_send(), 0)
     each(lambda k: chi_copy(k).wait_recv())
     total = part[pl.ds(pl.multiple_of(me * out_rows, out_rows), out_rows), :]
     for k in range(1, n):
@@ -358,6 +370,7 @@
     aux = three_center.shape[2]
     width = BS * BS // n
     chunk = 32
+    pieces = 4
     slot_of_block = invert(block_of_slot)
     keep = green_mask.astype(jnp.bfloat16)[0, :, None, None]
     occ = green_occ.reshape(KG, BS // 2, 2, BS // 2, 2).transpose(0, 2, 1, 4, 3)
@@ -382,15 +395,14 @@
             pltpu.VMEM((KN, aux, BS * BS), jnp.bfloat16),
             pltpu.VMEM((KN, aux, BS * BS), jnp.bfloat16),
             pltpu.VMEM((KN, aux, BS * BS), jnp.bfloat16),
-            pltpu.VMEM((n, KN, aux // 2, width), jnp.bfloat16),
-            pltpu.VMEM((n, KN, aux // 2, width), jnp.bfloat16),
             pltpu.VMEM((aux, aux), jnp.float32),
             pltpu.VMEM((n, aux // n, aux), jnp.float32),
         ]
-        + [sems((n,))] * 10
-        + [
-            sems((3,)),
-        ],
+        + [sems((n,))] * 2
+        + [sems((pieces, n))] * 6
+        + [sems((n,))] * 2
+        + [sems((1,)), sems((pieces,)), sems((pieces,))]
+        + [pltpu.VMEM((n, KN, aux // 2 // pieces, width), jnp.bfloat16)] * (2 * pieces),
         compiler_params=pltpu.CompilerParams(
             collective_id=0, has_side_effects=True, vmem_limit_bytes=48 * 1024 * 1024
         ),

time: 240 us -> 238 us (level)
  no operation moved by 1% of the time
where the time goes in v4:
time: 238 us
  Pallas kernels  227 us (95%)
  local copies, waits for them, and re-layouts  8.75 us (4%)
    pallas_call x1, Pallas kernels, by_row_slices(): pl.pallas_call(functools.partial(whole_kernel, n, chunk), out_shape=jax.S...  227 us

profile of v4, /device:TPU:0, one launch (start us, length us, event | category | flops | bytes accessed | tf_op | source)
XLA Modules:
  0.0 237.9 jit_solution(2839781323456137067)
XLA Ops:
  0.0 4.2 %reshape.12 = bf16[3,32,2,32,2]{4,3,2,1,0:T(8,128)(2,1)S(1)} reshape(bf16[1,3,4096]{2,1,0:T(4,128)(2,1)} %param.8) | data formatting | bytes 49152 | tf_op jit(solution)/shard_map/reshape | solution.py:376
  4.2 1.4 copy.10
  5.6 0.1 reshape.22
  5.7 0.9 concatenate.12
  6.6 0.7 convert_bitcast_fusion
  7.2 0.1 mul.16
  7.3 0.1 mul.17
  7.4 0.1 maximum_multiply_fusion
  7.5 0.7 convert_element_type.9
  8.2 0.7 compare_select_fusion
  8.8 0.8 scatter_custom_fusion.slots_ref
  9.6 0.0 copy-start
  9.6 0.6 copy-done
  10.3 227.0 %polarizability.1 = f32[16,256]{1,0:T(8,128)S(1)} custom-call(s32[16]{0:T(128)S(1)} %copy-done, s32[16]{0:T(128)S(1)} %scatter_custom_fusion.slots_ref, bf16[208,128]{1,0:T(8,128)(2,1)S(1)} %fusion.1.pack_ref, bf16[1,3,256,4096]{3,2,1,0:T(8,128)(2,1)} %tensor_ref.1), custom_call_target="tpu_custom_call" | custom-call | tf_op jit(solution)/shard_map/polarizability/pallas_call | solution.py:385
  237.3 0.6 copy.13
  (2 shorter events, 0.0 us)
Async XLA Ops:
  9.6 0.7 copy-start

commit v5 on v4

--- a/solution.py
+++ b/solution.py
@@ -303,10 +303,13 @@
 
         each(act, 0, piece // chunk)
 
+    def mixed(act):
+        each(lambda k: act(lax.rem(7 * k, n)))
+
     greet(n, me)
     each(lambda k: pack_copy(k).start())
     for p in range(pieces):
-        each(lambda k: tensor_copy(p, k).start())
+        mixed(lambda k: tensor_copy(p, k).start())
         own_tensor(p).start()
     own_pack = pltpu.make_async_copy(pack_ref, every.at[me], own_sem.at[0])
     own_pack.start()
@@ -324,14 +327,14 @@
     for p in range(pieces):
         own_tensor(p).wait()
         each(lambda k: tensor_copy(p, k).wait_recv())
-        each(lambda k: stage_and_send(p, k))
+        mixed(lambda k: stage_and_send(p, k))
         stage(p, 0)
         own_back(p).start()
         each(own_left, p * per_piece, (p + 1) * per_piece)
     for p in range(pieces):
         own_back(p).wait()
         pass_copy(p, 0).start()
-        each(lambda k: hand_on(p, k))
+        mixed(lambda k: hand_on(p, k))
         after_left(grp * half + p * piece)
     for p in range(pieces):
         each(lambda k: pass_copy(p, k).wait_recv(), 0)

time: 238 us -> 234 us (0.983)
  Pallas kernels: 227 us -> 223 us
    pallas_call x1, Pallas kernels: 227 us -> 223 us  [by_row_slices(): pl.pallas_call(functools.partial(whole_kernel, n, chunk), out_shape=jax.S...]
where the time goes in v5:
time: 234 us
  Pallas kernels  223 us (95%)
  local copies, waits for them, and re-layouts  8.75 us (4%)
    pallas_call x1, Pallas kernels, by_row_slices(): pl.pallas_call(functools.partial(whole_kernel, n, chunk), out_shape=jax.S...  223 us

profile of v5, /device:TPU:0, one launch (start us, length us, event | category | flops | bytes accessed | tf_op | source)
XLA Modules:
  0.0 233.7 jit_solution(4964569805996140887)
XLA Ops:
  0.0 4.2 %reshape.12 = bf16[3,32,2,32,2]{4,3,2,1,0:T(8,128)(2,1)S(1)} reshape(bf16[1,3,4096]{2,1,0:T(4,128)(2,1)} %param.8) | data formatting | bytes 49152 | tf_op jit(solution)/shard_map/reshape | solution.py:379
  4.2 1.4 copy.10
  5.6 0.1 reshape.22
  5.7 0.9 concatenate.12
  6.6 0.7 convert_bitcast_fusion
  7.2 0.1 mul.16
  7.3 0.1 mul.17
  7.4 0.1 maximum_multiply_fusion
  7.5 0.7 convert_element_type.9
  8.2 0.7 compare_select_fusion
  8.8 0.8 scatter_custom_fusion.slots_ref
  9.6 0.0 copy-start
  9.6 0.6 copy-done
  10.3 222.8 %polarizability.1 = f32[16,256]{1,0:T(8,128)S(1)} custom-call(s32[16]{0:T(128)S(1)} %copy-done, s32[16]{0:T(128)S(1)} %scatter_custom_fusion.slots_ref, bf16[208,128]{1,0:T(8,128)(2,1)S(1)} %fusion.1.pack_ref, bf16[1,3,256,4096]{3,2,1,0:T(8,128)(2,1)} %tensor_ref.1), custom_call_target="tpu_custom_call" | custom-call | tf_op jit(solution)/shard_map/polarizability/pallas_call | solution.py:388
  233.1 0.6 copy.13
  (2 shorter events, 0.0 us)
Async XLA Ops:
  9.6 0.7 copy-start
